TPU v7x, 128 devices: a whole 4x4x4 slice. The times are simulated.
128 devices in a mesh: row: 8 (over y, core), col: 16 (over z, x).
Axes of the slice: x: 4, y: 4, z: 4, core: 2. Of those that a mesh axis runs over, the one named last changes fastest.
Arguments:
- sigma_top: float32 [6144, 6144], P('row', 'col')
- factor_cross: float32 [6144, 6144], P('row', 'col'), may hold values from -0.078125 to 0.078125
- factor_inverse: float32 [6144, 6144], P('row', 'col')
- block_inverse: float32 [6144, 6144], P('row', 'col')
- ancestors: int32 [12], replicated, may hold values from 0 to 23, as said below
Outputs:
- sigma_cross: float32 [6144, 6144], P('row', 'col')
- sigma_child: float32 [6144, 6144], P('row', 'col')
Inputs may be any that keep to these rules, and one draw needn't show every extreme that they name: `ancestors`: 12 distinct block numbers; block 0 and block 23 are always among them.
All inputs are finite; a program needn't handle non-finite values.
Results may differ from a plain program's by a relative error of at most 0.000078.
Values sent between devices are 32-bit elements; how exact they have to be, the bound alone decides.
No kernel may reach another device: no remote copies, remote signals or barrier semaphores. Data moves between devices by JAX's collectives and lax.ppermute only.
A program may use at most 128 MiB of HBM per device.

v0:
```python
import jax
import jax.numpy as jnp
from jax import lax
from jax.sharding import PartitionSpec as P

BLK = 256


def transposed_rows(gathered, right_side):
    return lax.dot_general(
        gathered,
        right_side,
        (((0,), (0,)), ((), ())),
        precision=lax.Precision.HIGHEST,
        preferred_element_type=jnp.float32,
    )


def per_device(sigma_top, factor_cross, factor_inverse, block_inverse, ancestors):
    height = sigma_top.shape[0]
    first_row = lax.axis_index("row") * height
    blocks = (first_row + lax.iota(jnp.int32, height)) // BLK
    living = jnp.any(blocks[:, None] == ancestors[None, :], axis=1)
    masked = jnp.where(living[:, None], factor_cross, jnp.float32(0.0))
    inverse_strip = lax.all_gather(factor_inverse, "row", axis=0, tiled=True)
    rows_used = inverse_strip
    update = jnp.dot(
        lax.all_gather(masked, "col", axis=1, tiled=True),
        rows_used,
        precision=lax.Precision.HIGHEST,
        preferred_element_type=jnp.float32,
    )
    update_strip = lax.all_gather(update, "row", axis=0, tiled=True)
    rows_used = update_strip
    product = jnp.dot(
        lax.all_gather(sigma_top, "col", axis=1, tiled=True),
        rows_used,
        precision=lax.Precision.HIGHEST,
        preferred_element_type=jnp.float32,
    )
    sigma_cross = jnp.where(living[:, None], -product, jnp.float32(0.0))
    gathered = lax.all_gather(sigma_cross, "col", axis=1, tiled=True)
    correction = lax.psum_scatter(
        transposed_rows(gathered, update), "row", scatter_dimension=0, tiled=True
    )
    sigma_child = block_inverse - correction
    return (sigma_cross, sigma_child)


def solution(mesh):
    return jax.shard_map(
        per_device,
        mesh=mesh,
        in_specs=(P("row", "col"), P("row", "col"), P("row", "col"), P("row", "col"), P()),
        out_specs=(P("row", "col"), P("row", "col")),
        check_vma=False,
    )
```

profile of v0, /device:TPU:1, one launch (start us, length us, event | category | flops | bytes accessed | tf_op | source)
XLA Modules:
  0.0 643.4 jit_solution(8413906918570889155)
XLA Ops:
  7.2 0.0 all-gather.8.cloned.1.call-start
  7.2 0.7 all-gather.8.cloned.1.call-update
  7.9 0.0 all-gather.6.cloned.1.call-start
  8.0 0.7 compare_reduce_fusion
  8.7 2.5 broadcast_select_fusion
  11.2 0.0 all-gather.6.cloned.1.call-update
  11.2 0.0 all-gather.12.cloned.1.call-start
  11.2 0.7 all-gather.12.cloned.1.call-update
  11.9 0.0 all-gather.10.cloned.1.call-start
  12.0 55.5 %all-gather.8.cloned.1.call-done = f32[6144,384]{1,0:T(8,128)} async-done(((f32[768,384]{1,0:T(8,128)}), f32[6144,384]{1,0:T(8,128)}) %all-gather.8.cloned.1.call-update) | async-done | bytes 9437200 | tf_op jit(solution)/shard_map/all_gather | solution.py:25
  67.5 124.8 %all-gather.6.cloned.1.call-done = f32[768,6144]{1,0:T(8,128)} async-done(((f32[768,384]{1,0:T(8,128)}), f32[768,6144]{1,0:T(8,128)}) %all-gather.6.cloned.1.call-update) | async-done | bytes 18874384 | tf_op jit(solution)/shard_map/all_gather | solution.py:28
  192.3 34.1 %fusion.5 = f32[768,384]{1,0:T(8,128)} fusion(f32[768,6144]{1,0:T(8,128)} %all-gather.6.cloned.1.call-done, f32[6144,384]{1,0:T(8,128)} %all-gather.8.cloned.1.call-done), kind=kOutput, calls=%fused_computation.14 | convolution fusion | flops 21743271936 | bytes 29491200 | tf_op jit(solution)/shard_map/dot_general | solution.py:27
  226.4 0.0 all-gather.10.cloned.1.call-update
  226.4 0.0 copy-start
  226.4 0.2 all-gather.14.cloned.1.call-start
  226.6 89.7 %all-gather.12.cloned.1.call-done = f32[768,6144]{1,0:T(8,128)} async-done(((f32[768,384]{1,0:T(8,128)}), f32[768,6144]{1,0:T(8,128)}) %all-gather.12.cloned.1.call-update) | async-done | bytes 18874384 | tf_op jit(solution)/shard_map/all_gather | solution.py:36
  316.3 56.3 %all-gather.10.cloned.1.call-done = f32[6144,384]{1,0:T(8,128)} async-done(((f32[768,384]{1,0:T(8,128)}), f32[6144,384]{1,0:T(8,128)}) %all-gather.10.cloned.1.call-update) | async-done | bytes 9437200 | tf_op jit(solution)/shard_map/all_gather | solution.py:33
  372.6 48.7 %fusion.1 = f32[768,384]{0,1:T(8,128)} fusion(f32[6144,384]{1,0:T(8,128)} %all-gather.10.cloned.1.call-done, f32[768,6144]{1,0:T(8,128)} %all-gather.12.cloned.1.call-done, pred[768]{0:T(1024)(128)(4,1)S(1)} %compare_reduce_fusion), kind=kOutput, calls=%fused_computation.2 | convolution fusion | flops 21743861760 | bytes 29491968 | tf_op jit(solution)/shard_map/dot_general | solution.py:35
  421.3 0.0 all-gather.14.cloned.1.call-update
  421.3 0.3 reduce-scatter.2.cloned.1.call-start
  421.6 121.8 %all-gather.14.cloned.1.call-done = f32[768,6144]{0,1:T(8,128)} async-done(((f32[768,384]{0,1:T(8,128)}), f32[768,6144]{0,1:T(8,128)}) %all-gather.14.cloned.1.call-update) | async-done | bytes 18874384 | tf_op jit(solution)/shard_map/all_gather | solution.py:42
  543.4 0.0 copy-done
  543.4 34.0 %fusion.6 = f32[6144,384]{1,0:T(8,128)} fusion(f32[768,6144]{0,1:T(8,128)} %all-gather.14.cloned.1.call-done, f32[768,384]{1,0:T(8,128)S(1)} %copy-done), kind=kOutput, calls=%fused_computation.15 | convolution fusion | flops 21743271936 | bytes 29491200 | tf_op jit(solution)/shard_map/dot_general | solution.py:10
  577.5 0.0 copy-start.1
  577.5 0.0 copy-start.2
  577.5 0.0 reduce-scatter.2.cloned.1.call-update
  577.5 1.2 copy-done.1
  578.8 1.4 copy.8
  580.2 54.0 %reduce-scatter.2.cloned.1.call-done = f32[768,384]{1,0:T(8,128)} async-done(((f32[6144,384]{1,0:T(8,128)}), f32[768,384]{1,0:T(8,128)}) %reduce-scatter.2.cloned.1.call-update) | async-done | bytes 1179664 | tf_op jit(solution)/shard_map/reduce_scatter | solution.py:43
  634.2 0.0 copy-done.2
  634.2 2.4 sub.10
  (1 shorter events, 0.0 us)
Async XLA Ops:
  7.2 60.3 %all-gather.8.cloned.1.call-start = ((), (), s32[]{:S(2)}) async-start(), calls=%async_computation.2 | async-start | bytes 10616832 | tf_op jit(solution)/shard_map/all_gather | solution.py:25
  7.9 184.4 %all-gather.6.cloned.1.call-start = ((), (), s32[]{:S(2)}) async-start(), calls=%async_computation.1 | async-start | bytes 20054016 | tf_op jit(solution)/shard_map/all_gather | solution.py:28
  11.2 305.1 %all-gather.12.cloned.1.call-start = ((), (), s32[]{:S(2)}) async-start(), calls=%async_computation.4 | async-start | bytes 20054016 | tf_op jit(solution)/shard_map/all_gather | solution.py:36
  11.9 360.6 %all-gather.10.cloned.1.call-start = ((), (), s32[]{:S(2)}) async-start(), calls=%async_computation.3 | async-start | bytes 10616832 | tf_op jit(solution)/shard_map/all_gather | solution.py:33
  226.4 317.1 %copy-start = (f32[768,384]{1,0:T(8,128)S(1)}, f32[768,384]{1,0:T(8,128)}, u32[]{:S(2)}) copy-start(f32[768,384]{1,0:T(8,128)} %fusion.5) | copy-start | bytes 3538948
  226.4 317.0 %all-gather.14.cloned.1.call-start = ((), (), s32[]{:S(2)}) async-start(), calls=%async_computation.5 | async-start | bytes 20054016 | tf_op jit(solution)/shard_map/all_gather | solution.py:42
  421.3 212.8 %reduce-scatter.2.cloned.1.call-start = ((), (), s32[]{:S(2)}) async-start(), calls=%async_computation.6 | async-start | bytes 10616832 | tf_op jit(solution)/shard_map/reduce_scatter | solution.py:43
  577.5 1.3 copy-start.1
  577.5 56.7 %copy-start.2 = (f32[768,384]{1,0:T(8,128)S(1)}, f32[768,384]{1,0:T(8,128)}, u32[]{:S(2)}) copy-start(f32[768,384]{1,0:T(8,128)} %param.8) | copy-start | bytes 3538948
Sparse Core Ops, SparseCore 0:
  9.7 57.7 all-gather.7
  70.3 121.9 all-gather.5
  194.5 121.7 all-gather.11
  318.4 54.1 all-gather.9
  421.5 121.9 all-gather.13
  577.6 56.4 reduce-scatter.1
where the time goes:
time: 644 us; the launch traced here: 643 us
  waiting for transfers between devices  504 us (78%)
  matrix products  117 us (18%)
  between operations  14.1 us (2%)
    all_gather x1, waiting for transfers between devices, per_device(): lax.all_gather(masked, 'col', axis=1, tiled=True)  125 us
    all_gather x1, waiting for transfers between devices, per_device(): gathered = lax.all_gather(sigma_cross, 'col', axis=1, tiled=True)  122 us
    all_gather x1, waiting for transfers between devices, per_device(): lax.all_gather(sigma_top, 'col', axis=1, tiled=True)  89.7 us
    all_gather x1, waiting for transfers between devices, per_device(): update_strip = lax.all_gather(update, 'row', axis=0, tiled=True)  56.3 us
    all_gather x1, waiting for transfers between devices, per_device(): inverse_strip = lax.all_gather(factor_inverse, 'row', axis=0, tiled=True)  55.5 us
    reduce_scatter x1, waiting for transfers between devices, per_device(): lax.psum_scatter(transposed_rows(gathered, update), 'row', scatter_dimens...  54 us
    dot_general x1, matrix products, per_device(): jnp.dot(lax.all_gather(sigma_top, 'col', axis=1, tiled=True), rows_used,...  48.7 us
    dot_general x1, matrix products, per_device(): jnp.dot(lax.all_gather(masked, 'col', axis=1, tiled=True), rows_used, pre...  34.1 us
  transfers between devices with their start and end apart: 6, of which 6 were waited for; matrix products, arithmetic and copies ran while one was open for 6% of the time, Pallas kernels for 0%

commit v1 on v0

--- a/solution.py
+++ b/solution.py
@@ -1,9 +1,36 @@
+import functools
 import jax
 import jax.numpy as jnp
 from jax import lax
 from jax.sharding import PartitionSpec as P
 
 BLK = 256
+
+
+def finish_the_meshes(vector, axis_key):
+    mixed_arr = lax.psum(1, axis_key)
+    ready = lax.axis_index(axis_key)
+    side_arr, long_array, local_part = (mixed_arr, ready, vector.shape[1])
+    by_rank = [(i0, (i0 + 1) % side_arr) for i0 in range(side_arr)]
+    chunks = [(i0, (i0 - 1) % side_arr) for i0 in range(side_arr)]
+    f_next = jnp.zeros((*vector.shape[:1], side_arr * local_part, *vector.shape[2:]), vector.dtype)
+    f_next = lax.dynamic_update_slice_in_dim(f_next, vector, long_array * local_part, axis=1)
+    right_arr = even = vector
+    met_up = side_arr // 2
+    for jj in range(1, met_up + 1):
+        right_arr = lax.ppermute(right_arr, axis_key, by_rank)
+        f_next = lax.dynamic_update_slice_in_dim(
+            f_next, right_arr, (long_array - jj) % side_arr * local_part, axis=1
+        )
+        if jj < side_arr - met_up:
+            even = lax.ppermute(even, axis_key, chunks)
+            f_next = lax.dynamic_update_slice_in_dim(
+                f_next, even, (long_array + jj) % side_arr * local_part, axis=1
+            )
+    return f_next
+
+
+search_classes = functools.partial(finish_the_meshes, axis_key="col")
 
 
 def transposed_rows(gathered, right_side):
@@ -25,7 +52,7 @@
     inverse_strip = lax.all_gather(factor_inverse, "row", axis=0, tiled=True)
     rows_used = inverse_strip
     update = jnp.dot(
-        lax.all_gather(masked, "col", axis=1, tiled=True),
+        search_classes(masked),
         rows_used,
         precision=lax.Precision.HIGHEST,
         preferred_element_type=jnp.float32,

time: 644 us -> 728 us (1.13)
  local copies, waits for them, and re-layouts: 2.64 us -> 38.5 us
  starting transfers between devices: 0.64 us -> 34.3 us
  waiting for transfers between devices: 504 us -> 519 us
    ppermute x0 -> x15, waiting for transfers between devices: none -> 161 us  [the longest x8 161 us: finish_the_meshes(): right_arr = lax.ppermute(right_arr, axis_key, by_rank)]
    all_gather x1 -> x0, waiting for transfers between devices: 125 us -> none  [per_device(): lax.all_gather(masked, 'col', axis=1, tiled=True)]
    all_gather x1, waiting for transfers between devices: 55.5 us -> 0.01 us  [per_device(): inverse_strip = lax.all_gather(factor_inverse, 'row', axis=0, tiled=True)]
    all_gather x1, waiting for transfers between devices: 89.7 us -> 124 us  [per_device(): lax.all_gather(sigma_top, 'col', axis=1, tiled=True)]
    ppermute x0 -> x15, starting transfers between devices: none -> 33.6 us  [the longest x7 31.5 us: finish_the_meshes(): even = lax.ppermute(even, axis_key, chunks)]
    dynamic_update_slice x0 -> x15, local copies, waits for them, and re-layouts: none -> 25 us  [the longest x8 13.1 us: finish_the_meshes(): lax.dynamic_update_slice_in_dim(f_next, right_arr, (long_array - jj) % si...]
    broadcast_in_dim x0 -> x1, local copies, waits for them, and re-layouts: none -> 8.79 us  [finish_the_meshes(): jnp.zeros((*vector.shape[:1], side_arr * local_part, *vector.shape[2:]),...]
  transfers between devices with their start and end apart: 6 -> 20, of which waited for: 6 -> 12; matrix products, arithmetic and copies ran while one was open for 6% -> 5% of each run, Pallas kernels for 0% -> 0%
where the time goes in v1:
time: 728 us; the launch traced here: 727 us
  waiting for transfers between devices  519 us (71%)
  matrix products  117 us (16%)
  local copies, waits for them, and re-layouts  38.5 us (5%)
  starting transfers between devices  34.3 us (5%)
  between operations  13.9 us (2%)
    ppermute x8, waiting for transfers between devices, finish_the_meshes(): right_arr = lax.ppermute(right_arr, axis_key, by_rank)  161 us
    all_gather x1, waiting for transfers between devices, per_device(): lax.all_gather(sigma_top, 'col', axis=1, tiled=True)  124 us
    all_gather x1, waiting for transfers between devices, per_device(): gathered = lax.all_gather(sigma_cross, 'col', axis=1, tiled=True)  122 us
    all_gather x1, waiting for transfers between devices, per_device(): update_strip = lax.all_gather(update, 'row', axis=0, tiled=True)  57.1 us
    reduce_scatter x1, waiting for transfers between devices, per_device(): lax.psum_scatter(transposed_rows(gathered, update), 'row', scatter_dimens...  54 us
    dot_general x1, matrix products, per_device(): jnp.dot(lax.all_gather(sigma_top, 'col', axis=1, tiled=True), rows_used,...  48.7 us
    dot_general x1, matrix products, per_device(): jnp.dot(search_classes(masked), rows_used, precision=lax.Precision.HIGHES...  34.1 us
    dot_general x1, matrix products, transposed_rows(): lax.dot_general(gathered, right_side, (((0,), (0,)), ((), ())), precision...  34 us
  transfers between devices with their start and end apart: 20, of which 12 were waited for; matrix products, arithmetic and copies ran while one was open for 5% of the time, Pallas kernels for 0%

profile of v1, /device:TPU:1, one launch (start us, length us, event | category | flops | bytes accessed | tf_op | source)
XLA Modules:
  0.0 727.4 jit_solution(13319183504225935358)
XLA Ops:
  7.2 0.0 all-gather.5.cloned.1.call-start
  7.2 0.7 all-gather.5.cloned.1.call-update
  7.9 0.0 all-gather.7.cloned.1.call-start
  8.0 0.7 compare_reduce_fusion
  8.7 8.8 %broadcast_in_dim.28 = f32[768,6144]{1,0:T(8,128)} broadcast(f32[]{:T(128)} %constant.115.clone.1), dimensions={} | broadcast | bytes 18874372 | tf_op jit(solution)/shard_map/broadcast_in_dim | solution.py:16
  17.5 1.3 constant_dynamic-update-slice_fusion.15
  18.8 2.0 collective-permute-start
  20.8 4.7 collective-permute-start.1
  25.6 25.7 %collective-permute-done = f32[768,384]{1,0:T(8,128)S(1)} collective-permute-done((f32[768,384]{1,0:T(8,128)S(1)}, f32[768,384]{1,0:T(8,128)S(1)}, u32[]{:S(2)}, u32[]{:S(2)}) %collective-permute-start) | collective-permute-done | bytes 1179680 | tf_op jit(solution)/shard_map/ppermute | solution.py:21
  51.2 0.0 collective-permute-done.1
  51.2 4.8 collective-permute-start.3
  56.0 24.8 %collective-permute-done.2 = f32[768,384]{1,0:T(8,128)S(1)} collective-permute-done((f32[768,384]{1,0:T(8,128)S(1)}, f32[768,384]{1,0:T(8,128)S(1)}, u32[]{:S(2)}, u32[]{:S(2)}) %collective-permute-start.2) | collective-permute-done | bytes 1179680 | tf_op jit(solution)/shard_map/ppermute | solution.py:21
  80.8 0.0 copy-start.10
  80.8 4.8 collective-permute-start.5
  85.6 23.8 %collective-permute-done.4 = f32[768,384]{1,0:T(8,128)S(1)} collective-permute-done((f32[768,384]{1,0:T(8,128)S(1)}, f32[768,384]{1,0:T(8,128)S(1)}, u32[]{:S(2)}, u32[]{:S(2)}) %collective-permute-start.4) | collective-permute-done | bytes 1179680 | tf_op jit(solution)/shard_map/ppermute | solution.py:21
  109.4 0.0 collective-permute-done.5
  109.4 4.8 collective-permute-start.7
  114.2 22.9 %collective-permute-done.6 = f32[768,384]{1,0:T(8,128)S(1)} collective-permute-done((f32[768,384]{1,0:T(8,128)S(1)}, f32[768,384]{1,0:T(8,128)S(1)}, u32[]{:S(2)}, u32[]{:S(2)}) %collective-permute-start.6) | collective-permute-done | bytes 1179680 | tf_op jit(solution)/shard_map/ppermute | solution.py:21
  137.1 0.0 collective-permute-start.8
  137.1 0.0 collective-permute-done.7
  137.2 1.0 copy-done.3
  138.2 3.8 collective-permute-start.9
  142.0 21.9 %collective-permute-done.8 = f32[768,384]{1,0:T(8,128)S(1)} collective-permute-done((f32[768,384]{1,0:T(8,128)S(1)}, f32[768,384]{1,0:T(8,128)S(1)}, u32[]{:S(2)}, u32[]{:S(2)}) %collective-permute-start.8) | collective-permute-done | bytes 1179680 | tf_op jit(solution)/shard_map/ppermute | solution.py:21
  163.9 0.0 collective-permute-start.10
  164.0 1.0 copy-done.11
  165.0 3.8 collective-permute-start.11
  168.8 21.1 %collective-permute-done.10 = f32[768,384]{1,0:T(8,128)} collective-permute-done((f32[768,384]{1,0:T(8,128)S(1)}, f32[768,384]{1,0:T(8,128)}, u32[]{:S(2)}, u32[]{:S(2)}) %collective-permute-start.10) | collective-permute-done | bytes 1179680 | tf_op jit(solution)/shard_map/ppermute | solution.py:21
  189.9 1.1 constant_dynamic-update-slice_fusion.14
  191.0 1.1 constant_dynamic-update-slice_fusion.13
  192.2 2.4 constant_dynamic-update-slice_fusion.12
  194.6 2.4 constant_dynamic-update-slice_fusion.11
  197.1 4.8 collective-permute-start.13
  201.9 1.2 constant_dynamic-update-slice_fusion.10
  203.1 12.0 %collective-permute-done.12 = f32[768,384]{1,0:T(8,128)} collective-permute-done((f32[768,384]{1,0:T(8,128)}, f32[768,384]{1,0:T(8,128)}, u32[]{:S(2)}, u32[]{:S(2)}) %collective-permute-start.12) | collective-permute-done | bytes 1179680 | tf_op jit(solution)/shard_map/ppermute | solution.py:21
  215.2 0.0 collective-permute-start.14
  215.2 1.2 constant_dynamic-update-slice_fusion.9
  216.3 1.2 constant_dynamic-update-slice_fusion.8
  217.6 1.2 constant_dynamic-update-slice_fusion.7
  218.7 1.1 constant_dynamic-update-slice_fusion.6
  219.9 2.5 constant_dynamic-update-slice_fusion.5
  222.3 2.4 constant_dynamic-update-slice_fusion.4
  224.8 2.4 constant_dynamic-update-slice_fusion.3
  227.2 2.4 constant_dynamic-update-slice_fusion.2
  229.6 1.1 constant_dynamic-update-slice_fusion.1
  230.7 8.7 %collective-permute-done.14 = f32[768,384]{1,0:T(8,128)S(1)} collective-permute-done((f32[768,384]{1,0:T(8,128)}, f32[768,384]{1,0:T(8,128)S(1)}, u32[]{:S(2)}, u32[]{:S(2)}) %collective-permute-start.14) | collective-permute-done | bytes 1179680 | tf_op jit(solution)/shard_map/ppermute | solution.py:21
  239.4 1.1 constant_dynamic-update-slice_fusion
  240.6 34.1 %fusion.5 = f32[768,384]{1,0:T(8,128)} fusion(f32[768,6144]{1,0:T(8,128)} %constant_dynamic-update-slice_fusion, f32[6144,384]{1,0:T(8,128)} %all-gather.5.cloned.1.call-done), kind=kOutput, calls=%fused_computation.30 | convolution fusion | flops 21743271936 | bytes 29491200 | tf_op jit(solution)/shard_map/dot_general | solution.py:54
  274.7 0.0 all-gather.7.cloned.1.call-update
  274.7 0.0 all-gather.9.cloned.1.call-start
  274.7 0.7 all-gather.9.cloned.1.call-update
  275.4 0.0 copy-start
  275.4 0.3 all-gather.11.cloned.1.call-start
  275.7 57.1 %all-gather.7.cloned.1.call-done = f32[6144,384]{1,0:T(8,128)} async-done(((f32[768,384]{1,0:T(8,128)}), f32[6144,384]{1,0:T(8,128)}) %all-gather.7.cloned.1.call-update) | async-done | bytes 9437200 | tf_op jit(solution)/shard_map/all_gather | solution.py:60
  332.8 124.2 %all-gather.9.cloned.1.call-done = f32[768,6144]{1,0:T(8,128)} async-done(((f32[768,384]{1,0:T(8,128)}), f32[768,6144]{1,0:T(8,128)}) %all-gather.9.cloned.1.call-update) | async-done | bytes 18874384 | tf_op jit(solution)/shard_map/all_gather | solution.py:63
  457.1 48.7 %fusion.1 = f32[768,384]{0,1:T(8,128)} fusion(f32[6144,384]{1,0:T(8,128)} %all-gather.7.cloned.1.call-done, f32[768,6144]{1,0:T(8,128)} %all-gather.9.cloned.1.call-done, pred[768]{0:T(1024)(128)(4,1)S(1)} %compare_reduce_fusion), kind=kOutput, calls=%fused_computation.2 | convolution fusion | flops 21743861760 | bytes 29491968 | tf_op jit(solution)/shard_map/dot_general | solution.py:62
  505.8 0.0 all-gather.11.cloned.1.call-update
  505.8 0.3 reduce-scatter.2.cloned.1.call-start
  506.1 121.6 %all-gather.11.cloned.1.call-done = f32[768,6144]{0,1:T(8,128)} async-done(((f32[768,384]{0,1:T(8,128)}), f32[768,6144]{0,1:T(8,128)}) %all-gather.11.cloned.1.call-update) | async-done | bytes 18874384 | tf_op jit(solution)/shard_map/all_gather | solution.py:69
  627.7 34.0 %fusion.6 = f32[6144,384]{1,0:T(8,128)} fusion(f32[768,6144]{0,1:T(8,128)} %all-gather.11.cloned.1.call-done, f32[768,384]{1,0:T(8,128)S(1)} %copy-done), kind=kOutput, calls=%fused_computation.31 | convolution fusion | flops 21743271936 | bytes 29491200 | tf_op jit(solution)/shard_map/dot_general | solution.py:37
  661.8 0.0 reduce-scatter.2.cloned.1.call-update
  661.8 1.2 copy-done.1
  663.0 1.4 copy.8
  664.4 54.0 %reduce-scatter.2.cloned.1.call-done = f32[768,384]{1,0:T(8,128)} async-done(((f32[6144,384]{1,0:T(8,128)}), f32[768,384]{1,0:T(8,128)}) %reduce-scatter.2.cloned.1.call-update) | async-done | bytes 1179664 | tf_op jit(solution)/shard_map/reduce_scatter | solution.py:70
  718.4 2.4 sub.42
  (33 shorter events, 0.1 us)
Async XLA Ops:
  7.2 233.4 %all-gather.5.cloned.1.call-start = ((), (), s32[]{:S(2)}) async-start(), calls=%async_computation.1 | async-start | bytes 10616832 | tf_op jit(solution)/shard_map/all_gather | solution.py:52
  7.9 324.9 %all-gather.7.cloned.1.call-start = ((), (), s32[]{:S(2)}) async-start(), calls=%async_computation.2 | async-start | bytes 10616832 | tf_op jit(solution)/shard_map/all_gather | solution.py:60
  8.7 8.8 %copy-start.13 = (f32[768,384]{1,0:T(8,128)S(1)}, f32[768,384]{1,0:T(8,128)}, u32[]{:S(2)}) copy-start(f32[768,384]{1,0:T(8,128)} %param.6) | copy-start | bytes 3538948
  18.8 32.4 %collective-permute-start = (f32[768,384]{1,0:T(8,128)S(1)}, f32[768,384]{1,0:T(8,128)S(1)}, u32[]{:S(2)}, u32[]{:S(2)}) collective-permute-start(f32[768,384]{1,0:T(8,128)S(1)} %get-tuple-element.7), channel_id=1, source_target_pairs={{0,1},{1,2},{2,3},{3,4},{4,5},{5,6},{6,7},{7,8},{8,9},{9,10},{10,1... | collective-permute-start | bytes 3538952 | tf_op jit(solution)/shard_map/ppermute | solution.py:21
  20.8 30.4 %collective-permute-start.1 = (f32[768,384]{1,0:T(8,128)S(1)}, f32[768,384]{1,0:T(8,128)S(1)}, u32[]{:S(2)}, u32[]{:S(2)}) collective-permute-start(f32[768,384]{1,0:T(8,128)S(1)} %get-tuple-element.7), channel_id=1, source_target_pairs={{0,15},{1,0},{2,1},{3,2},{4,3},{5,4},{6,5},{7,6},{8,7},{9,8},{10,9... | collective-permute-start | bytes 3538952 | tf_op jit(solution)/shard_map/ppermute | solution.py:26
  51.2 29.6 %collective-permute-start.2 = (f32[768,384]{1,0:T(8,128)S(1)}, f32[768,384]{1,0:T(8,128)S(1)}, u32[]{:S(2)}, u32[]{:S(2)}) collective-permute-start(f32[768,384]{1,0:T(8,128)S(1)} %collective-permute-done), channel_id=1, source_target_pairs={{0,1},{1,2},{2,3},{3,4},{4,5},{5,6},{6,7},{7,8},{8,9},{9,10},{10,1... | collective-permute-start | bytes 3538952 | tf_op jit(solution)/shard_map/ppermute | solution.py:21
  51.2 29.6 %collective-permute-start.3 = (f32[768,384]{1,0:T(8,128)S(1)}, f32[768,384]{1,0:T(8,128)S(1)}, u32[]{:S(2)}, u32[]{:S(2)}) collective-permute-start(f32[768,384]{1,0:T(8,128)S(1)} %collective-permute-done.1), channel_id=1, source_target_pairs={{0,15},{1,0},{2,1},{3,2},{4,3},{5,4},{6,5},{7,6},{8,7},{9,8},{10,9... | collective-permute-start | bytes 3538952 | tf_op jit(solution)/shard_map/ppermute | solution.py:26
  80.8 4.8 copy-start.5
  80.8 28.6 %collective-permute-start.4 = (f32[768,384]{1,0:T(8,128)S(1)}, f32[768,384]{1,0:T(8,128)S(1)}, u32[]{:S(2)}, u32[]{:S(2)}) collective-permute-start(f32[768,384]{1,0:T(8,128)S(1)} %collective-permute-done.2), channel_id=1, source_target_pairs={{0,1},{1,2},{2,3},{3,4},{4,5},{5,6},{6,7},{7,8},{8,9},{9,10},{10,1... | collective-permute-start | bytes 3538952 | tf_op jit(solution)/shard_map/ppermute | solution.py:21
  80.8 28.6 %copy-start.10 = (f32[768,384]{1,0:T(8,128)}, f32[768,384]{1,0:T(8,128)S(1)}, u32[]{:S(2)}) copy-start(f32[768,384]{1,0:T(8,128)S(1)} %collective-permute-done.3) | copy-start | bytes 3538948
  80.8 28.6 %collective-permute-start.5 = (f32[768,384]{1,0:T(8,128)S(1)}, f32[768,384]{1,0:T(8,128)S(1)}, u32[]{:S(2)}, u32[]{:S(2)}) collective-permute-start(f32[768,384]{1,0:T(8,128)S(1)} %collective-permute-done.3), channel_id=1, source_target_pairs={{0,15},{1,0},{2,1},{3,2},{4,3},{5,4},{6,5},{7,6},{8,7},{9,8},{10,9... | collective-permute-start | bytes 3538952 | tf_op jit(solution)/shard_map/ppermute | solution.py:26
  109.4 54.5 %copy-start.6 = (f32[768,384]{1,0:T(8,128)}, f32[768,384]{1,0:T(8,128)S(1)}, u32[]{:S(2)}) copy-start(f32[768,384]{1,0:T(8,128)S(1)} %collective-permute-done.4) | copy-start | bytes 3538948
  109.4 27.7 %collective-permute-start.6 = (f32[768,384]{1,0:T(8,128)S(1)}, f32[768,384]{1,0:T(8,128)S(1)}, u32[]{:S(2)}, u32[]{:S(2)}) collective-permute-start(f32[768,384]{1,0:T(8,128)S(1)} %collective-permute-done.4), channel_id=1, source_target_pairs={{0,1},{1,2},{2,3},{3,4},{4,5},{5,6},{6,7},{7,8},{8,9},{9,10},{10,1... | collective-permute-start | bytes 3538952 | tf_op jit(solution)/shard_map/ppermute | solution.py:21
  109.4 27.7 %collective-permute-start.7 = (f32[768,384]{1,0:T(8,128)S(1)}, f32[768,384]{1,0:T(8,128)S(1)}, u32[]{:S(2)}, u32[]{:S(2)}) collective-permute-start(f32[768,384]{1,0:T(8,128)S(1)} %collective-permute-done.5), channel_id=1, source_target_pairs={{0,15},{1,0},{2,1},{3,2},{4,3},{5,4},{6,5},{7,6},{8,7},{9,8},{10,9... | collective-permute-start | bytes 3538952 | tf_op jit(solution)/shard_map/ppermute | solution.py:26
  137.1 1.0 copy-start.3
  137.1 26.8 %collective-permute-start.8 = (f32[768,384]{1,0:T(8,128)S(1)}, f32[768,384]{1,0:T(8,128)S(1)}, u32[]{:S(2)}, u32[]{:S(2)}) collective-permute-start(f32[768,384]{1,0:T(8,128)S(1)} %collective-permute-done.6), channel_id=1, source_target_pairs={{0,1},{1,2},{2,3},{3,4},{4,5},{5,6},{6,7},{7,8},{8,9},{9,10},{10,1... | collective-permute-start | bytes 3538952 | tf_op jit(solution)/shard_map/ppermute | solution.py:21
  138.2 25.8 %copy-start.8 = (f32[768,384]{1,0:T(8,128)}, f32[768,384]{1,0:T(8,128)S(1)}, u32[]{:S(2)}) copy-start(f32[768,384]{1,0:T(8,128)S(1)} %collective-permute-done.7) | copy-start | bytes 3538948
  138.2 25.8 %collective-permute-start.9 = (f32[768,384]{1,0:T(8,128)S(1)}, f32[768,384]{1,0:T(8,128)}, u32[]{:S(2)}, u32[]{:S(2)}) collective-permute-start(f32[768,384]{1,0:T(8,128)S(1)} %collective-permute-done.7), channel_id=1, source_target_pairs={{0,15},{1,0},{2,1},{3,2},{4,3},{5,4},{6,5},{7,6},{8,7},{9,8},{10,9... | collective-permute-start | bytes 3538952 | tf_op jit(solution)/shard_map/ppermute | solution.py:26
  163.9 1.0 copy-start.11
  163.9 26.0 %collective-permute-start.10 = (f32[768,384]{1,0:T(8,128)S(1)}, f32[768,384]{1,0:T(8,128)}, u32[]{:S(2)}, u32[]{:S(2)}) collective-permute-start(f32[768,384]{1,0:T(8,128)S(1)} %collective-permute-done.8), channel_id=1, source_target_pairs={{0,1},{1,2},{2,3},{3,4},{4,5},{5,6},{6,7},{7,8},{8,9},{9,10},{10,1... | collective-permute-start | bytes 3538952 | tf_op jit(solution)/shard_map/ppermute | solution.py:21
  165.0 32.1 %collective-permute-start.11 = (f32[768,384]{1,0:T(8,128)}, f32[768,384]{1,0:T(8,128)}, u32[]{:S(2)}, u32[]{:S(2)}) collective-permute-start(f32[768,384]{1,0:T(8,128)} %collective-permute-done.9), channel_id=1, source_target_pairs={{0,15},{1,0},{2,1},{3,2},{4,3},{5,4},{6,5},{7,6},{8,7},{9,8},{10,9... | collective-permute-start | bytes 3538952 | tf_op jit(solution)/shard_map/ppermute | solution.py:26
  189.9 25.3 %collective-permute-start.12 = (f32[768,384]{1,0:T(8,128)}, f32[768,384]{1,0:T(8,128)}, u32[]{:S(2)}, u32[]{:S(2)}) collective-permute-start(f32[768,384]{1,0:T(8,128)} %collective-permute-done.10), channel_id=1, source_target_pairs={{0,1},{1,2},{2,3},{3,4},{4,5},{5,6},{6,7},{7,8},{8,9},{9,10},{10,1... | collective-permute-start | bytes 3538952 | tf_op jit(solution)/shard_map/ppermute | solution.py:21
  189.9 12.0 %copy-start.7 = (f32[768,384]{1,0:T(8,128)S(1)}, f32[768,384]{1,0:T(8,128)}, u32[]{:S(2)}) copy-start(f32[768,384]{1,0:T(8,128)} %copy-done.6) | copy-start | bytes 3538948
  189.9 26.4 %copy-start.4 = (f32[768,384]{1,0:T(8,128)S(1)}, f32[768,384]{1,0:T(8,128)}, u32[]{:S(2)}) copy-start(f32[768,384]{1,0:T(8,128)} %copy-done.3) | copy-start | bytes 3538948
  189.9 27.7 %copy-start.9 = (f32[768,384]{1,0:T(8,128)S(1)}, f32[768,384]{1,0:T(8,128)}, u32[]{:S(2)}) copy-start(f32[768,384]{1,0:T(8,128)} %copy-done.8) | copy-start | bytes 3538948
  189.9 28.8 %copy-start.12 = (f32[768,384]{1,0:T(8,128)S(1)}, f32[768,384]{1,0:T(8,128)}, u32[]{:S(2)}) copy-start(f32[768,384]{1,0:T(8,128)} %copy-done.11) | copy-start | bytes 3538948
  197.1 32.5 %collective-permute-start.13 = (f32[768,384]{1,0:T(8,128)}, f32[768,384]{1,0:T(8,128)S(1)}, u32[]{:S(2)}, u32[]{:S(2)}) collective-permute-start(f32[768,384]{1,0:T(8,128)} %collective-permute-done.11), channel_id=1, source_target_pairs={{0,15},{1,0},{2,1},{3,2},{4,3},{5,4},{6,5},{7,6},{8,7},{9,8},{10,9... | collective-permute-start | bytes 3538952 | tf_op jit(solution)/shard_map/ppermute | solution.py:26
  215.2 24.3 %collective-permute-start.14 = (f32[768,384]{1,0:T(8,128)}, f32[768,384]{1,0:T(8,128)S(1)}, u32[]{:S(2)}, u32[]{:S(2)}) collective-permute-start(f32[768,384]{1,0:T(8,128)} %collective-permute-done.12), channel_id=1, source_target_pairs={{0,1},{1,2},{2,3},{3,4},{4,5},{5,6},{6,7},{7,8},{8,9},{9,10},{10,1... | collective-permute-start | bytes 3538952 | tf_op jit(solution)/shard_map/ppermute | solution.py:21
  274.7 182.4 %all-gather.9.cloned.1.call-start = ((), (), s32[]{:S(2)}) async-start(), calls=%async_computation.3 | async-start | bytes 20054016 | tf_op jit(solution)/shard_map/all_gather | solution.py:63
  275.4 352.3 %copy-start = (f32[768,384]{1,0:T(8,128)S(1)}, f32[768,384]{1,0:T(8,128)}, u32[]{:S(2)}) copy-start(f32[768,384]{1,0:T(8,128)} %fusion.5) | copy-start | bytes 3538948
  275.4 352.3 %all-gather.11.cloned.1.call-start = ((), (), s32[]{:S(2)}) async-start(), calls=%async_computation.4 | async-start | bytes 20054016 | tf_op jit(solution)/shard_map/all_gather | solution.py:69
  505.8 212.6 %reduce-scatter.2.cloned.1.call-start = ((), (), s32[]{:S(2)}) async-start(), calls=%async_computation.5 | async-start | bytes 10616832 | tf_op jit(solution)/shard_map/reduce_scatter | solution.py:70
  661.8 1.3 copy-start.1
  661.8 56.7 %copy-start.2 = (f32[768,384]{1,0:T(8,128)S(1)}, f32[768,384]{1,0:T(8,128)}, u32[]{:S(2)}) copy-start(f32[768,384]{1,0:T(8,128)} %param.8) | copy-start | bytes 3538948
Sparse Core Ops, SparseCore 0:
  9.7 57.7 all-gather.4
  274.8 57.9 all-gather.6
  335.0 121.9 all-gather.8
  506.0 121.7 all-gather.10
  661.9 56.4 reduce-scatter.1
